TPU v7x, 32 devices: a whole 2x2x4 slice. The times are simulated.
32 devices in a mesh: blk: 8 (over y, x, core), docs: 4 (over z).
Axes of the slice: x: 2, y: 2, z: 4, core: 2. Of those that a mesh axis runs over, the one named last changes fastest.
Arguments:
- acts: bfloat16 [16384, 4096], P(('blk', 'docs')), may hold values from -6 to 6
- grads: bfloat16 [16384, 7168], P(('blk', 'docs')), may hold values from -6 to 6
- proj_in: bfloat16 [4096, 64], replicated, may hold values from -0.09375 to 0.09375
- proj_out: bfloat16 [7168, 64], replicated, may hold values from -0.0625 to 0.0625
- doc_ids: int32 [16384], P('blk'), may hold values from 0 to 511, as said below
- doc_slot: int32 [512], replicated, may hold values from 0 to 511, as said below
- train_grads: bfloat16 [32768, 4096], P(('blk', 'docs')), may hold values from -0.09375 to 0.09375
- train_scale: float32 [32768], P(('blk', 'docs')), may hold values from 0.5 to 4
Outputs:
- scores: float32 [512, 32768], P(None, ('blk', 'docs'))
Inputs may be any that keep to these rules, and one draw needn't show every extreme that they name: `doc_ids`: tokens of group b (rows b * 2048 to (b + 1) * 2048 - 1) name only documents b * 64 to (b + 1) * 64 - 1; each document is one contiguous run of 16 or more tokens, a multiple of 16 long, and every document is named. `doc_slot`: within each group b, documents b * 64 to (b + 1) * 64 - 1 take the slots b * 64 to (b + 1) * 64 - 1, each once; slot s is owned by docs index (s // 16) % 4.
All inputs are finite; a program needn't handle non-finite values.
Results may differ from a plain program's by a relative error of at most 0.005.
Values may be sent and summed in bfloat16 or wider, within the bound.
A program may use at most 128 MiB of HBM per device.

v0:
```python
import jax
import jax.numpy as jnp
from jax import lax
from jax.sharding import PartitionSpec as P

DOC_DEV = 16


def outer_sum(left_rows, right_rows, slots, targets):
    width = left_rows.shape[1]
    count = left_rows.shape[0]
    owners = (slots[:, None] == targets[None, :]).astype(jnp.bfloat16)
    weighted = (owners[:, :, None] * right_rows[:, None, :]).reshape(
        count, targets.shape[0] * width
    )
    return lax.dot_general(
        weighted, left_rows, (((0,), (0,)), ((), ())), preferred_element_type=jnp.float32
    )


def body(acts, grads, proj_in, proj_out, doc_ids, doc_slot, train_grads, train_scale):
    width = proj_in.shape[1]
    left_rows = jnp.dot(acts, proj_in, preferred_element_type=jnp.float32).astype(jnp.bfloat16)
    right_rows = jnp.dot(grads, proj_out, preferred_element_type=jnp.float32).astype(jnp.bfloat16)
    group_docs = DOC_DEV * lax.axis_size("docs")
    group_slots = jnp.take(doc_slot, doc_ids) % group_docs
    member = lax.axis_index("docs")
    packed = jnp.concatenate([left_rows, right_rows], axis=1)
    owned_ids = member * DOC_DEV + jnp.arange(DOC_DEV, dtype=jnp.int32)
    block_rows = lax.all_gather(packed, "docs", axis=0, tiled=True)
    sums = outer_sum(block_rows[:, :width], block_rows[:, width:], group_slots, owned_ids)
    owned = sums.reshape(DOC_DEV, width * width).astype(jnp.bfloat16)
    grouped = lax.all_gather(owned, "docs", axis=0, tiled=True)
    product = lax.dot_general(
        lax.all_gather(grouped, "blk", axis=0, tiled=True),
        train_grads,
        (((1,), (1,)), ((), ())),
        preferred_element_type=jnp.float32,
    )
    return product * train_scale[None, :]


def solution(mesh):
    placed = (
        P(("blk", "docs"), None),
        P(("blk", "docs"), None),
        P(),
        P(),
        P("blk"),
        P(),
        P(("blk", "docs"), None),
        P(("blk", "docs")),
    )
    return jax.shard_map(
        body, mesh=mesh, in_specs=placed, out_specs=P(None, ("blk", "docs")), check_vma=False
    )
```

profile of v0, /device:TPU:17, one launch (start us, length us, event | category | flops | bytes accessed | tf_op | source)
XLA Modules:
  0.0 119.8 jit_solution(6001954080863332782)
XLA Ops:
  6.5 0.0 copy-start
  6.5 0.0 copy-start.1
  6.5 0.0 all-gather.2.cloned.1.call-start
  6.5 0.8 fusion.2
  7.3 0.0 copy-done.1
  7.3 0.0 copy-start.3
  7.3 0.0 copy-start.2
  7.4 13.2 %gather_fusion = s32[2048]{0:T(1024)S(1)} fusion(s32[512]{0:T(512)S(1)} %copy-done.1, s32[2048]{0:T(1024)S(1)} %fusion.2), kind=kCustom, calls=%fused_computation | custom fusion | bytes 24576 | tf_op jit(solution)/shard_map/jit(_take)/gather | solution.py:26
  20.6 0.0 copy-done.3
  20.6 0.0 copy-done.2
  20.6 3.6 %convolution_convert_fusion.2 = bf16[512,64]{0,1:T(8,128)(2,1)S(1)} fusion(bf16[512,4096]{1,0:T(8,128)(2,1)} %param.8, bf16[4096,64]{0,1:T(8,128)(2,1)S(1)} %copy-done.2), kind=kOutput, calls=%fused_computation.5 | convolution fusion | flops 268468224 | bytes 4784128 | tf_op jit(solution)/shard_map/dot_general | solution.py:23
  24.2 0.0 copy-done
  24.2 5.4 %convolution_convert_fusion.1 = bf16[512,64]{0,1:T(8,128)(2,1)S(1)} fusion(bf16[512,7168]{1,0:T(8,128)(2,1)} %param.9, bf16[7168,64]{0,1:T(8,128)(2,1)S(1)} %copy-done), kind=kOutput, calls=%fused_computation.4 | convolution fusion | flops 469794816 | bytes 8323072 | tf_op jit(solution)/shard_map/dot_general | solution.py:24
  29.6 12.8 %all_gather.9 = bf16[2048,128]{0,1:T(8,128)(2,1)S(1)} all-gather(bf16[512,128]{0,1:T(8,128)(2,1)S(1)} %pad_maximum_fusion), channel_id=1, replica_groups=mesh['blk'=8,'docs'=4] {'docs'}, dimensions={0}, use_global_device_ids=true | all-gather | bytes 655360 | tf_op jit(solution)/shard_map/all_gather | solution.py:30
  42.5 0.1 compare_convert_fusion
  42.5 0.3 broadcast_multiply_fusion
  42.9 0.0 copy-start.4
  42.9 1.4 %convolution_convert_fusion = bf16[1024,64]{0,1:T(8,128)(2,1)S(1)} fusion(bf16[2048,1024]{0,1:T(8,128)(2,1)S(1)} %bitcast.8, bf16[2048,128]{0,1:T(8,128)(2,1)S(1)} %all_gather.9), kind=kOutput, calls=%fused_computation.3 | convolution fusion | flops 268500992 | bytes 4587520 | tf_op jit(solution)/shard_map/dot_general | solution.py:16
  44.3 0.2 copy.10
  44.5 0.3 convert_element_type.23
  44.8 12.4 %all_gather.10 = bf16[64,4096]{1,0:T(8,128)(2,1)} all-gather(bf16[16,4096]{1,0:T(8,128)(2,1)S(1)} %convert_element_type.23), channel_id=1, replica_groups=mesh['blk'=8,'docs'=4] {'docs'}, dimensions={0}, use_global_device_ids=true | all-gather | bytes 655360 | tf_op jit(solution)/shard_map/all_gather | solution.py:33
  57.2 0.0 all-gather.2.cloned.1.call-update
  57.2 45.2 %all-gather.2.cloned.1.call-done = bf16[512,4096]{1,0:T(8,128)(2,1)} async-done(((bf16[64,4096]{1,0:T(8,128)(2,1)}), bf16[512,4096]{1,0:T(8,128)(2,1)}) %all-gather.2.cloned.1.call-update) | async-done | bytes 4194320 | tf_op jit(solution)/shard_map/all_gather | solution.py:35
  102.4 0.0 copy-done.4
  102.4 10.5 %convolution_multiply_fusion = f32[512,1024]{1,0:T(8,128)} fusion(bf16[512,4096]{1,0:T(8,128)(2,1)} %all-gather.2.cloned.1.call-done, bf16[1024,4096]{1,0:T(8,128)(2,1)} %param.14, f32[1024]{0:T(1024)S(1)} %copy-done.4), kind=kOutput, calls=%fused_computation.2 | convolution fusion | flops 4295491584 | bytes 14684160 | tf_op jit(solution)/shard_map/dot_general | solution.py:34
  (4 shorter events, 0.0 us)
Async XLA Ops:
  6.5 17.7 %copy-start = (bf16[7168,64]{0,1:T(8,128)(2,1)S(1)}, bf16[7168,64]{0,1:T(8,128)(2,1)}, u32[]{:S(2)}) copy-start(bf16[7168,64]{0,1:T(8,128)(2,1)} %param.11) | copy-start | bytes 2752516
  6.5 0.8 copy-start.1
  6.5 95.9 %all-gather.2.cloned.1.call-start = ((), (), s32[]{:S(2)}) async-start(), calls=%async_computation | async-start | bytes 4718592 | tf_op jit(solution)/shard_map/all_gather | solution.py:35
  7.3 13.2 %copy-start.3 = (s32[2048]{0:T(1024)S(1)}, s32[2048]{0:T(1024)}, u32[]{:S(2)}) copy-start(s32[2048]{0:T(1024)} %param.12) | copy-start | bytes 24580
  7.3 13.3 %copy-start.2 = (bf16[4096,64]{0,1:T(8,128)(2,1)S(1)}, bf16[4096,64]{0,1:T(8,128)(2,1)}, u32[]{:S(2)}) copy-start(bf16[4096,64]{0,1:T(8,128)(2,1)} %param.10) | copy-start | bytes 1572868
  42.9 59.5 %copy-start.4 = (f32[1024]{0:T(1024)S(1)}, f32[1024]{0:T(1024)}, u32[]{:S(2)}) copy-start(f32[1024]{0:T(1024)} %param.15) | copy-start | bytes 12292
Sparse Core Ops, SparseCore 0:
  57.3 45.0 all-gather.1
where the time goes:
time: 121 us; the launch traced here: 120 us
  waiting for transfers between devices  45.2 us (37%)
  blocking collectives  25.2 us (21%)
  matrix products  20.9 us (17%)
  local copies, waits for them, and re-layouts  13.7 us (11%)
  between operations  13.5 us (11%)
  other arithmetic  1.24 us (1%)
    all_gather x1, waiting for transfers between devices, body(): lax.all_gather(grouped, 'blk', axis=0, tiled=True)  45.2 us
    gather x1, local copies, waits for them, and re-layouts, body(): group_slots = jnp.take(doc_slot, doc_ids) % group_docs  13.2 us
    all_gather x1, blocking collectives, body(): block_rows = lax.all_gather(packed, 'docs', axis=0, tiled=True)  12.8 us
    all_gather x1, blocking collectives, body(): grouped = lax.all_gather(owned, 'docs', axis=0, tiled=True)  12.4 us
    dot_general x1, matrix products, body(): lax.dot_general(lax.all_gather(grouped, 'blk', axis=0, tiled=True), train...  10.5 us
    dot_general x1, matrix products, body(): jnp.dot(grads, proj_out, preferred_element_type=jnp.float32)  5.43 us
    dot_general x1, matrix products, body(): jnp.dot(acts, proj_in, preferred_element_type=jnp.float32)  3.58 us
  transfers between devices with their start and end apart: 1, of which 1 were waited for; matrix products, arithmetic and copies ran while one was open for 0% of the time, Pallas kernels for 0%

commit v1 on v0

v1 whole, which is shorter than its diff:
```python
import functools

import jax
import jax.numpy as jnp
from jax import lax
from jax.experimental import pallas as pl
from jax.experimental.pallas import tpu as pltpu
from jax.sharding import PartitionSpec as P

RUN = 16
CLS = 4
PARTS = 2
F32 = jnp.float32
BF16 = jnp.bfloat16


def flip(value, step):
    return value + (1 - 2 * ((value // step) % 2)) * step


def xor(a, b, bits):
    return sum(((((a // (1 << k)) % 2) + ((b // (1 << k)) % 2)) % 2) * (1 << k) for k in range(bits))


def kernel(nb, nq, group_docs, acts, grads, pin, pout, slots, train, out,
           a_v, g_v, t_v, rt_v, gat, blocks, prod, mask_l, load_sem, t_sem, send_sem, recv_sem):
    b, d = lax.axis_index("blk"), lax.axis_index("docs")
    chip, core = b // 2, b % 2
    chips = nb // 2
    bits = chips.bit_length() - 1
    tok = acts.shape[0]
    width = pin.shape[1]
    half = tok // 2
    pairs = width // 2
    nd = tok // RUN // CLS
    part = tok // PARTS

    loads = []
    for p in range(PARTS):
        rows = pl.ds(p * part, part)
        loads.append((
            pltpu.make_async_copy(acts.at[rows], a_v.at[rows], load_sem.at[2 * p]),
            pltpu.make_async_copy(grads.at[rows], g_v.at[rows], load_sem.at[2 * p + 1]),
        ))
    for one, two in loads:
        one.start()
        two.start()
    t_copy = pltpu.make_async_copy(train, t_v, t_sem)
    t_copy.start()

    sibling = (flip(b, 1), d)
    partners = [(flip(b, 2 << k), d) for k in range(bits)]
    peers = [(b, lax.rem(d + k, nq)) for k in range(1, nq)]
    barrier = pltpu.get_barrier_semaphore()
    for who in [sibling] + partners + peers:
        pl.semaphore_signal(barrier, inc=1, device_id=who, device_id_type=pl.DeviceIdType.MESH)

    t_id = lax.broadcasted_iota(jnp.int32, (tok, CLS * width), 0)
    l_id = lax.broadcasted_iota(jnp.int32, (tok, CLS * width), 1)
    cls, at = (t_id // RUN) % CLS, l_id // width
    mask_l[0] = (cls == at).astype(F32).astype(BF16)
    swapped = at + 1 - 2 * (at % 2)
    mask_l[1] = (cls == swapped).astype(F32).astype(BF16)

    lefts = []
    for p in range(PARTS):
        rows = pl.ds(p * part, part)
        loads[p][0].wait()
        lefts.append(jnp.dot(a_v[rows, :], pin[...], preferred_element_type=F32))
        loads[p][1].wait()
        right = jnp.dot(g_v[rows, :], pout[...], preferred_element_type=F32)
        turned = right.T
        for tb in range(part // 128):
            rt_v[pl.ds((p * part // 128 + tb) * width, width), :] = turned[:, tb * 128:(tb + 1) * 128]
    left = jnp.concatenate(lefts, axis=0)
    gat[0, 0, 0, pl.ds(0, half), :] = jnp.concatenate([left[:half], left[half:]], axis=1).astype(BF16)
    tiles = tok // 128
    for h in range(2):
        for tb in range(tiles):
            rows = rt_v[pl.ds(tb * width + h, pairs, stride=2), :].astype(BF16)
            gat[0, 0, 0, pl.ds(half + (h * tiles + tb) * pairs, pairs), :] = rows
    gat[0, 0, 0, pl.ds(tok, 16), :] = slots[...]

    pl.semaphore_wait(barrier, 1 + bits + nq - 1)

    sends = []

    def send(src, dst, who):
        index = len(sends)
        copy = pltpu.make_async_remote_copy(
            src_ref=gat.at[src], dst_ref=gat.at[dst],
            send_sem=send_sem.at[index], recv_sem=recv_sem.at[dst],
            device_id=who, device_id_type=pl.DeviceIdType.MESH)
        copy.start()
        sends.append(copy)

    def arrived(slot):
        pltpu.make_async_remote_copy(
            src_ref=gat.at[slot], dst_ref=gat.at[slot],
            send_sem=send_sem.at[0], recv_sem=recv_sem.at[slot],
            device_id=sibling, device_id_type=pl.DeviceIdType.MESH).wait_recv()

    def order(j):
        return list(range(bits)) if j % 2 == 0 else list(range(bits))[::-1]

    def spread(j, stage):
        o = order(j)
        if stage == 0:
            new = [0]
            if j:
                arrived((j, 0, 0))
        else:
            new = [0]
            for k in range(stage - 1):
                new = new + [r + (1 << o[k]) for r in new]
            new = [r + (1 << o[stage - 1]) for r in new]
            for r in new:
                arrived((j, r, 0))
        for k in range(stage, bits):
            for r in new:
                send((j, r, 0), (j, r + (1 << o[k]), 0), partners[o[k]])
        for r in new:
            send((j, r, 0), (j, r, 1), sibling)

    def first(j):
        spread(j, 0)

    def rest(j):
        for stage in range(1, bits + 1):
            spread(j, stage)
        for r in range(chips):
            arrived((j, r, 1))

    low = lax.broadcasted_iota(jnp.int32, (half, 2 * width), 1) < width
    low_p = lax.broadcasted_iota(jnp.int32, (pairs * nd, 2 * width), 1) < width
    d_id = lax.broadcasted_iota(jnp.int32, (nd, tok), 0)
    mask_d = (d_id == lax.broadcasted_iota(jnp.int32, (nd, tok), 1) // (RUN * CLS)).astype(F32)

    def outer(j):
        def pair(r, carry):
            results = []
            for a in range(2):
                slot = gat.at[j, r, lax.rem(core + a, 2)]
                packed = slot[pl.ds(0, half), :].astype(F32)
                turned = pltpu.roll(packed, width, 1)
                dup = jnp.concatenate([jnp.where(low, packed, turned), jnp.where(low, turned, packed)], axis=0).astype(BF16)
                wide = jnp.concatenate([dup] * (CLS // 2), axis=1)
                parts = []
                for h in range(2):
                    rt = jnp.concatenate(
                        [slot[pl.ds(half + (h * tiles + tb) * pairs, pairs), :] for tb in range(tiles)], axis=1).astype(F32)
                    lhs = (rt[:, None, :] * mask_d[None, :, :]).reshape(pairs * nd, tok).astype(BF16)
                    parts.append(jnp.dot(lhs, wide * mask_l[h], preferred_element_type=F32))
                results.append(parts)
            base = xor(chip, r, bits) * (2 * nd * CLS)
            for ch in range(CLS // 2):
                cols = slice(ch * 2 * width, (ch + 1) * 2 * width)
                for cl in range(2):
                    pieces = []
                    for a in range(2):
                        e, f = results[a][0][:, cols], results[a][1][:, cols]
                        if cl == 0:
                            pieces.append(jnp.where(low_p, e, f))
                        else:
                            pieces.append(pltpu.roll(jnp.where(low_p, f, e), width, 1))
                    at_row = pl.multiple_of(base + (ch * 2 + cl) * 2 * nd, 16)
                    for p in range(pairs):
                        rows = slice(p * nd, (p + 1) * nd)
                        tile = jnp.concatenate([pieces[0][rows], pieces[1][rows]], axis=0)
                        blocks[pl.ds(at_row, 2 * nd), pl.ds(p * 2 * width, 2 * width)] = tile.astype(BF16)
            return carry
        lax.fori_loop(0, chips, pair, 0)

    def finish(j):
        n_tile = 256
        four = 4 * group_docs
        per = 4 * nd * CLS

        def tile(n, carry):
            cols = pl.ds(pl.multiple_of(n * n_tile, n_tile), n_tile)
            prod[...] = lax.dot_general(blocks[...], t_v[cols, :], (((1,), (1,)), ((), ())), preferred_element_type=F32)

            def put(q4, c2):
                vec = jnp.zeros((1, 128), F32)
                for s in range(2):
                    r = xor(chip, q4 * 2 + s, bits)
                    for a in range(2):
                        vec = vec + gat[j, r, a, pl.ds(tok, 16), :].astype(F32)[0:1]
                lane = lax.broadcasted_iota(jnp.int32, (1, 128), 1)
                group = 2 * (lane // 64) + (lane % 16) // 8
                target = vec + (group * group_docs).astype(F32)
                row = lax.broadcasted_iota(jnp.int32, (four, 128), 0).astype(F32)
                pick = (row == target).astype(F32).astype(BF16)
                x = prod[pl.ds(pl.multiple_of(q4 * per, per), per), :]
                hi = x.astype(BF16)
                lo = (x - hi.astype(F32)).astype(BF16)
                add = jnp.dot(pick, hi, preferred_element_type=F32) + jnp.dot(pick, lo, preferred_element_type=F32)
                rows = pl.ds(pl.multiple_of(q4 * four, four), four)
                if j == 0:
                    out[rows, cols] = add
                else:
                    out[rows, cols] += add
                return c2
            return lax.fori_loop(0, chips // 2, put, carry)
        lax.fori_loop(0, train.shape[0] // n_tile, tile, 0)

    for k in range(1, nq):
        send((0, 0, 0), (k, 0, 0), peers[k - 1])
    first(0)
    for j in range(nq):
        if j + 1 < nq:
            first(j + 1)
        rest(j)
        outer(j)
        if j == 0:
            t_copy.wait()
        finish(j)
    for copy in sends:
        copy.wait_send()


def body(acts, grads, proj_in, proj_out, doc_ids, doc_slot, train_grads, train_scale):
    nb, nq = lax.axis_size("blk"), lax.axis_size("docs")
    b, d = lax.axis_index("blk"), lax.axis_index("docs")
    tok, width = acts.shape[0], proj_in.shape[1]
    docs = doc_slot.shape[0]
    group_docs = docs // nb
    chips = nb // 2
    bits = chips.bit_length() - 1
    nd = tok // RUN // CLS

    own = lax.dynamic_slice(doc_slot, (b * group_docs,), (group_docs,)) % group_docs
    ids = lax.dynamic_slice(doc_ids.reshape(-1, tok // RUN, RUN)[:, :, 0], (d, 0), (1, tok // RUN))[0] - b * group_docs
    ids = jnp.transpose(ids.reshape(nd, CLS)).reshape(CLS, 1, nd)
    found = jnp.sum(jnp.where(ids[..., None] == jnp.arange(group_docs), own, 0), axis=-1)
    here = ((jnp.arange(2)[:, None, None, None] == (b // 2) % 2) & (jnp.arange(2)[None, None, :, None] == b % 2))
    vec = jnp.where(here, found[None], 0).reshape(1, 4 * nd * CLS).astype(BF16)
    slots = jnp.broadcast_to(vec, (16, vec.shape[1]))

    rows = tok + 16
    n_sends = nq - 1 + nq * (chips - 1 + chips)
    any_spec = pl.BlockSpec(memory_space=pl.ANY)
    vmem = pl.BlockSpec(memory_space=pltpu.VMEM)
    product = pl.pallas_call(
        functools.partial(kernel, nb, nq, group_docs),
        out_shape=jax.ShapeDtypeStruct((docs, train_grads.shape[0]), F32),
        in_specs=[any_spec, any_spec, vmem, vmem, vmem, any_spec],
        out_specs=vmem,
        scratch_shapes=[
            pltpu.VMEM(acts.shape, BF16),
            pltpu.VMEM(grads.shape, BF16),
            pltpu.VMEM(train_grads.shape, BF16),
            pltpu.VMEM((tok // 128 * width, 128), F32),
            pltpu.VMEM((nq, chips, 2, rows, 128), BF16),
            pltpu.VMEM((nb * nd * CLS, width * width), BF16),
            pltpu.VMEM((nb * nd * CLS, 256), F32),
            pltpu.VMEM((2, tok, CLS * width), BF16),
            pltpu.SemaphoreType.DMA((2 * PARTS,)),
            pltpu.SemaphoreType.DMA,
            pltpu.SemaphoreType.DMA((n_sends,)),
            pltpu.SemaphoreType.DMA((nq, chips, 2)),
        ],
        compiler_params=pltpu.CompilerParams(
            collective_id=0, has_side_effects=True, vmem_limit_bytes=62 * 2**20),
        cost_estimate=pl.CostEstimate(flops=10**10, bytes_accessed=25 * 10**6, transcendentals=0),
    )(acts, grads, proj_in, proj_out, slots, train_grads)
    return product * train_scale[None, :]


def solution(mesh):
    placed = (
        P(("blk", "docs"), None),
        P(("blk", "docs"), None),
        P(),
        P(),
        P("blk"),
        P(),
        P(("blk", "docs"), None),
        P(("blk", "docs")),
    )
    return jax.shard_map(
        body, mesh=mesh, in_specs=placed, out_specs=P(None, ("blk", "docs")), check_vma=False
    )
```

time: 121 us -> 89.9 us (0.74)
  Pallas kernels: 0 us -> 79.3 us
  waiting for transfers between devices: 45.2 us -> 0 us
  blocking collectives: 25.2 us -> 0 us
  matrix products: 20.9 us -> 0 us
  between operations: 13.5 us -> 0.03 us
  local copies, waits for them, and re-layouts: 13.7 us -> 5.65 us
  other arithmetic: 1.24 us -> 4.62 us
    pallas_call x0 -> x1, Pallas kernels: none -> 79.3 us  [body(): pl.pallas_call(functools.partial(kernel, nb, nq, group_docs), out_shape=j...]
    all_gather x1 -> x0, waiting for transfers between devices: 45.2 us -> none  [body(): lax.all_gather(grouped, 'blk', axis=0, tiled=True)]
    all_gather x2 -> x0, blocking collectives: 25.2 us -> none  [the longest x1 12.8 us: body(): block_rows = lax.all_gather(packed, 'docs', axis=0, tiled=True)]
    dot_general x4 -> x0, matrix products: 20.9 us -> none  [the longest x1 10.5 us: body(): lax.dot_general(lax.all_gather(grouped, 'blk', axis=0, tiled=True), train...]
    gather x1 -> x0, local copies, waits for them, and re-layouts: 13.2 us -> none  [body(): group_slots = jnp.take(doc_slot, doc_ids) % group_docs]
    unnamed x10 -> x6, local copies, waits for them, and re-layouts: 0.02 us -> 4.01 us
    mul x1, other arithmetic: 0.34 us -> 3.27 us  [body(): return product * train_scale[None, :]]
  transfers between devices with their start and end apart: 1 -> 0, of which waited for: 1 -> 0; matrix products, arithmetic and copies ran while one was open for 0% -> 0% of each run, Pallas kernels for 0% -> 0%
where the time goes in v1:
time: 89.9 us; the launch traced here: 89.6 us
  Pallas kernels  79.3 us (88%)
  local copies, waits for them, and re-layouts  5.65 us (6%)
  other arithmetic  4.62 us (5%)
    pallas_call x1, Pallas kernels, body(): pl.pallas_call(functools.partial(kernel, nb, nq, group_docs), out_shape=j...  79.3 us
    unnamed x6, local copies, waits for them, and re-layouts  4.01 us
    mul x1, other arithmetic, body(): return product * train_scale[None, :]  3.27 us

profile of v1, /device:TPU:17, one launch (start us, length us, event | category | flops | bytes accessed | tf_op | source)
XLA Modules:
  0.0 89.6 jit_solution(9662610402090542587)
XLA Ops:
  0.0 0.0 copy-start
  0.0 0.8 and_select_fusion
  0.9 0.1 broadcast_and_fusion
  0.9 0.8 reshape.92
  1.7 0.1 subtract_reduce_fusion
  1.8 0.1 sub.17
  1.9 0.1 copy.15
  2.0 0.2 select_reduce_fusion
  2.2 0.1 select_convert_fusion
  2.3 0.1 convert_element_type.12
  2.4 0.6 broadcast_in_dim.43.slots
  3.0 2.4 %copy.16.pin = bf16[4096,64]{1,0:T(8,128)(2,1)} copy(bf16[4096,64]{0,1:T(8,128)(2,1)} %param.10) | data formatting | bytes 1048576 | tf_op args[2]
  5.4 0.0 copy-done
  5.4 1.6 %copy.17.pout = bf16[7168,64]{1,0:T(8,128)(2,1)} copy(bf16[7168,64]{0,1:T(8,128)(2,1)S(1)} %copy-done) | data formatting | bytes 1835008 | tf_op args[3]
  7.0 0.0 copy-start.1
  7.0 79.3 %shard_map.82 = f32[512,1024]{1,0:T(8,128)} custom-call(bf16[512,4096]{1,0:T(8,128)(2,1)} %acts.1, bf16[512,7168]{1,0:T(8,128)(2,1)} %grads.1, bf16[4096,64]{1,0:T(8,128)(2,1)} %copy.16.pin, bf16[7168,64]{1,0:T(8,128)(2,1)} %copy.17.pout, bf16[16,128]{1,0:T(8,128)(2,1)} %broadcast_in_dim.43.slots, bf16[1024,4096]{1,0:T(8,128)(2,1)} %train.1), custom_call_target="tpu_custom_call" | custom-call | flops 10000000000 | bytes 25000000 | tf_op jit(solution)/shard_map/pallas_call | solution.py:244
  86.3 0.0 copy-done.1
  86.3 3.3 %broadcast_multiply_fusion = f32[512,1024]{1,0:T(8,128)} fusion(f32[512,1024]{1,0:T(8,128)} %shard_map.82, f32[1024]{0:T(1024)S(1)} %copy-done.1), kind=kLoop, calls=%fused_computation | loop fusion | flops 524288 | bytes 4198400 | tf_op jit(solution)/shard_map/mul | solution.py:267
  (1 shorter events, 0.0 us)
Async XLA Ops:
  0.0 5.4 %copy-start = (bf16[7168,64]{0,1:T(8,128)(2,1)S(1)}, bf16[7168,64]{0,1:T(8,128)(2,1)}, u32[]{:S(2)}) copy-start(bf16[7168,64]{0,1:T(8,128)(2,1)} %param.11) | copy-start | bytes 2752516
  7.0 79.3 %copy-start.1 = (f32[1024]{0:T(1024)S(1)}, f32[1024]{0:T(1024)}, u32[]{:S(2)}) copy-start(f32[1024]{0:T(1024)} %param.15) | copy-start | bytes 12292
